TPU v7x, 32 devices: a whole 2x2x4 slice. The times are simulated.
32 devices in a mesh: seq: 2 (over x), exp: 8 (over z, core), dp: 2 (over y).
Axes of the slice: x: 2, y: 2, z: 4, core: 2. Of those that a mesh axis runs over, the one named last changes fastest.
Arguments:
- tokens: bfloat16 [16, 256, 2880], P(('exp', 'dp'), 'seq'), may hold values from -6 to 6
- segments: int32 [16, 256], P(('exp', 'dp')), may hold values from 0 to 1, as said below
- routes: int32 [16, 256, 4], P(('exp', 'dp'), 'seq'), may hold values from 0 to 7, all different within a row; in each aligned block of 128 rows (0 to 127, 128 to 255, ..., all dimensions but the last counted through in order) at most 72 rows name the same one
- gate_share: float32 [16, 256, 4], P(('exp', 'dp'), 'seq'), may hold values from 0.1 to 0.4
- attn_gain: float32 [2880], replicated, may hold values from 0.5 to 1.5
- query_weight: bfloat16 [2880, 4096], P(None, ('seq', 'exp', 'dp')), may hold values from -0.109375 to 0.109375
- query_bias: float32 [4096], replicated, may hold values from -1.8 to 1.8
- key_weight: bfloat16 [2880, 512], P(None, ('seq', 'exp', 'dp')), may hold values from -0.109375 to 0.109375
- key_bias: float32 [512], replicated, may hold values from -1.8 to 1.8
- value_weight: bfloat16 [2880, 512], P(None, ('seq', 'exp', 'dp')), may hold values from -0.109375 to 0.109375
- value_bias: float32 [512], replicated, may hold values from -1.8 to 1.8
- output_weight: bfloat16 [4096, 2880], P(('seq', 'exp', 'dp')), may hold values from -0.375 to 0.375
- output_bias: float32 [2880], replicated, may hold values from -1.8 to 1.8
- sink_logits: float32 [64], replicated, may hold values from -3 to 3
- moe_gain: float32 [2880], replicated, may hold values from 0.5 to 1.5
- gate_weight: bfloat16 [8, 2880, 2880], P('exp', None, ('seq', 'dp')), may hold values from -0.109375 to 0.109375
- gate_bias: float32 [8, 2880], P('exp', ('seq', 'dp')), may hold values from -0.6 to 0.6
- up_weight: bfloat16 [8, 2880, 2880], P('exp', None, ('seq', 'dp')), may hold values from -0.109375 to 0.109375
- up_bias: float32 [8, 2880], P('exp', ('seq', 'dp')), may hold values from -0.6 to 0.6
- down_weight: bfloat16 [8, 2880, 2880], P('exp', ('seq', 'dp')), may hold values from -0.109375 to 0.109375
- down_bias: float32 [8, 2880], P('exp'), may hold values from -0.6 to 0.6
- cotangent: bfloat16 [16, 256, 2880], P(('exp', 'dp'), 'seq'), may hold values from -6 to 6
Outputs:
- output: bfloat16 [16, 256, 2880], P(('exp', 'dp'), 'seq')
- input_grad: float32 [16, 256, 2880], P(('exp', 'dp'), 'seq')
- attn_gain_grad: float32 [2880], replicated
- query_weight_grad: float32 [2880, 4096], P(None, ('seq', 'exp', 'dp'))
- query_bias_grad: float32 [4096], replicated
- key_weight_grad: float32 [2880, 512], P(None, ('seq', 'exp', 'dp'))
- key_bias_grad: float32 [512], replicated
- value_weight_grad: float32 [2880, 512], P(None, ('seq', 'exp', 'dp'))
- value_bias_grad: float32 [512], replicated
- output_weight_grad: float32 [4096, 2880], P(('seq', 'exp', 'dp'))
- output_bias_grad: float32 [2880], replicated
- sink_grad: float32 [64], replicated
- moe_gain_grad: float32 [2880], replicated
- gate_weight_grad: float32 [8, 2880, 2880], P('exp', None, ('seq', 'dp'))
- gate_bias_grad: float32 [8, 2880], P('exp', ('seq', 'dp'))
- up_weight_grad: float32 [8, 2880, 2880], P('exp', None, ('seq', 'dp'))
- up_bias_grad: float32 [8, 2880], P('exp', ('seq', 'dp'))
- down_weight_grad: float32 [8, 2880, 2880], P('exp', ('seq', 'dp'))
- down_bias_grad: float32 [8, 2880], P('exp')
Inputs may be any that keep to these rules, and one draw needn't show every extreme that they name: `segments`: along a sequence the numbers never fall; equal numbers mark one document. `routes`: each token names 4 different experts; among the tokens of one device no expert is named by more than 72 of them.
All inputs are finite; a program needn't handle non-finite values.
Results may differ from a plain program's by a relative error of at most 0.02.
Values may be sent and summed in bfloat16 or wider, within the bound.
A program may use at most 512 MiB of HBM per device.

v0:
```python
import math

import jax
import jax.numpy as jnp
from jax import lax
from jax.experimental import pallas as pl
from jax.experimental.pallas import tpu as pltpu
from jax.sharding import PartitionSpec as P

HD = 64


highest = lax.Precision.HIGHEST
norm_eps = 1e-05
rope_base = 150000.0
clip_level = 7.0
glu_alpha = 1.702
masked_score = -1000000000.0


def rms_apply(values, gain):
    return values * lax.rsqrt(jnp.mean(values * values, axis=-1, keepdims=True) + norm_eps) * gain


def rope_tables(position, width):
    exponent = jnp.arange(width // 2).astype(jnp.float32) * (2.0 / width)
    freqs = jnp.exp(-math.log(rope_base) * exponent)
    angles = position.astype(jnp.float32)[:, None] * freqs[None, :]
    return (jnp.cos(angles), jnp.sin(angles))


def rotate(values, cosine, sine):
    half = values.shape[-1] // 2
    first = values[..., :half]
    second = values[..., half:]
    return jnp.concatenate(
        [first * cosine - second * sine, second * cosine + first * sine], axis=-1
    )


def swiglu(gate_pre, up_pre):
    gate_soft = clip_level * jnp.tanh(gate_pre / clip_level)
    up_soft = clip_level * jnp.tanh(up_pre / clip_level)
    return gate_soft * jax.nn.sigmoid(glu_alpha * gate_soft) * (up_soft + 1.0)


def inner_rows(left, right):
    return lax.dot_general(
        left, right, (((0,), (0,)), ((), ())), preferred_element_type=jnp.float32
    )


def times_transposed(left, right):
    return lax.dot_general(
        left, right, (((1,), (1,)), ((), ())), preferred_element_type=jnp.float32
    )


def to_experts(outgoing):
    width = outgoing.shape[2]
    arrived = lax.all_to_all(outgoing, "exp", split_axis=0, concat_axis=0, tiled=True)
    arrived = lax.all_gather(arrived, ("seq", "dp"), axis=0, tiled=True)
    return arrived.reshape(-1, width)


def results_back(activation, down_matrix, down_vector, experts, capacity):
    width = down_matrix.shape[1]
    share = lax.psum_scatter(
        jnp.dot(activation, down_matrix, preferred_element_type=jnp.float32).astype(jnp.bfloat16),
        ("seq", "dp"),
        scatter_dimension=0,
        tiled=True,
    ).astype(jnp.float32)
    finished = (share + down_vector).astype(jnp.bfloat16).reshape(experts, capacity, width)
    return lax.all_to_all(finished, "exp", split_axis=0, concat_axis=0, tiled=True)


def gradients_back(gate_grad, up_grad, gate_matrix, up_matrix, experts, capacity):
    share = lax.psum_scatter(
        times_transposed(gate_grad, gate_matrix) + times_transposed(up_grad, up_matrix),
        ("seq", "dp"),
        scatter_dimension=0,
        tiled=True,
    )
    return lax.all_to_all(
        share.reshape(experts, capacity, share.shape[1]),
        "exp",
        split_axis=0,
        concat_axis=0,
        tiled=True,
    )


def local(
    tokens,
    segments,
    routes,
    gate_share,
    attn_gain,
    query_weight,
    query_bias,
    key_weight,
    key_bias,
    value_weight,
    value_bias,
    output_weight,
    output_bias,
    sink_logits,
    moe_gain,
    gate_weight,
    gate_bias,
    up_weight,
    up_bias,
    down_weight,
    down_bias,
    cotangent,
):
    count_rows = tokens.shape[1]
    width = tokens.shape[2]
    head_count = sink_logits.shape[0]
    kv_count = key_bias.shape[0] // HD
    group = head_count // kv_count
    scale = 1.0 / math.sqrt(HD)
    experts = lax.axis_size("exp")
    topk = routes.shape[2]
    capacity = count_rows * topk * 9 // (8 * experts)
    resid = tokens[0].astype(jnp.float32)
    full_query, full_key, full_value, full_output = (
        lax.all_gather(query_weight, ("seq", "exp", "dp"), axis=1, tiled=True),
        lax.all_gather(key_weight, ("seq", "exp", "dp"), axis=1, tiled=True),
        lax.all_gather(value_weight, ("seq", "exp", "dp"), axis=1, tiled=True),
        lax.all_gather(output_weight, ("seq", "exp", "dp"), axis=0, tiled=True),
    )
    attn_norm, attn_norm_pull = jax.vjp(rms_apply, resid, attn_gain)
    normed = attn_norm.astype(jnp.bfloat16)
    query_lin = jnp.dot(normed, full_query, preferred_element_type=jnp.float32) + query_bias
    key_lin = jnp.dot(normed, full_key, preferred_element_type=jnp.float32) + key_bias
    value_low = (
        jnp.dot(normed, full_value, preferred_element_type=jnp.float32) + value_bias
    ).astype(jnp.bfloat16)
    offset = lax.axis_index("seq") * count_rows
    position = offset + jnp.arange(count_rows, dtype=jnp.int32)
    cosine, sine = rope_tables(position, HD)
    cosine = cosine[:, None]
    sine = sine[:, None]
    query_rot = rotate(query_lin.reshape(count_rows, head_count, HD), cosine, sine).astype(
        jnp.bfloat16
    )
    key_rot = rotate(key_lin.reshape(count_rows, kv_count, HD), cosine, sine).astype(jnp.bfloat16)
    all_keys, all_values = (
        lax.all_gather(key_rot.reshape(count_rows, kv_count * HD), "seq", axis=0, tiled=True),
        lax.all_gather(value_low, "seq", axis=0, tiled=True),
    )
    seq_len = all_keys.shape[0]
    all_keys = all_keys.reshape(seq_len, kv_count, HD)
    all_values = all_values.reshape(seq_len, kv_count, HD)
    doc_ids = segments[0]
    own_ids = lax.dynamic_slice_in_dim(doc_ids, offset, count_rows, 0)
    key_place = jnp.arange(seq_len, dtype=jnp.int32)
    visible = (position[:, None] >= key_place[None, :]) & (own_ids[:, None] == doc_ids[None, :])
    query_group = query_rot.reshape(count_rows, kv_count, group, HD)
    sink_grid = sink_logits.reshape(kv_count, group)[:, :, None]

    def score_block():
        raw = (
            jnp.einsum("qkgd,skd->kgqs", query_group, all_keys, preferred_element_type=jnp.float32)
            * scale
        )
        return jnp.where(visible[None, None], raw, masked_score)

    scores = score_block()
    peak = jnp.maximum(jnp.max(scores, axis=-1), sink_grid)
    total = jnp.sum(jnp.exp(scores - peak[..., None]), axis=-1) + jnp.exp(sink_grid - peak)
    log_total = peak + jnp.log(total)
    probs = jnp.exp(scores - log_total[..., None])
    mixed = jnp.einsum(
        "kgqs,skd->qkgd", probs.astype(jnp.bfloat16), all_values, preferred_element_type=jnp.float32
    )
    mixed = mixed.reshape(count_rows, head_count * HD).astype(jnp.bfloat16)
    attn_out = jnp.dot(mixed, full_output, preferred_element_type=jnp.float32) + output_bias
    hidden = resid + attn_out
    moe_norm, moe_norm_pull = jax.vjp(rms_apply, hidden, moe_gain)
    normed_moe = moe_norm.astype(jnp.bfloat16)
    chosen = routes[0].reshape(-1)
    expert_hot = (chosen[:, None] == jnp.arange(experts, dtype=jnp.int32)[None, :]).astype(
        jnp.int32
    )
    slot_index = jnp.sum((jnp.cumsum(expert_hot, axis=0) - expert_hot) * expert_hot, axis=1)
    target = chosen * capacity + slot_index
    slot_hot = (
        target[:, None] == jnp.arange(experts * capacity, dtype=jnp.int32)[None, :]
    ).reshape(count_rows, topk, experts * capacity)
    dispatch = jnp.sum(slot_hot.astype(jnp.bfloat16), axis=1)
    weighted = jnp.sum(slot_hot.astype(jnp.float32) * gate_share[0][:, :, None], axis=1)
    outgoing = jnp.einsum("ts,td->sd", dispatch, normed_moe, preferred_element_type=jnp.float32)
    outgoing = outgoing.astype(jnp.bfloat16).reshape(experts, capacity, width)
    expert_rows = to_experts(outgoing)
    gate_pre = (
        jnp.dot(expert_rows, gate_weight[0], preferred_element_type=jnp.float32) + gate_bias[0]
    )
    up_pre = jnp.dot(expert_rows, up_weight[0], preferred_element_type=jnp.float32) + up_bias[0]
    act_full, swiglu_pull = jax.vjp(swiglu, gate_pre, up_pre)
    activation = act_full.astype(jnp.bfloat16)
    returned = results_back(activation, down_weight[0], down_bias[0], experts, capacity)
    moe_out = jnp.dot(
        weighted, returned.reshape(experts * capacity, width).astype(jnp.float32), precision=highest
    )
    output = (hidden + moe_out).astype(jnp.bfloat16)
    upstream = cotangent[0].astype(jnp.float32)
    grad_slots = jnp.einsum("ts,td->sd", weighted, upstream, precision=highest)
    grad_slots = grad_slots.astype(jnp.bfloat16).reshape(experts, capacity, width)
    grad_rows = to_experts(grad_slots)
    down_bias_grad = jnp.sum(grad_rows.astype(jnp.float32), axis=0)
    down_weight_grad = inner_rows(activation, grad_rows)
    act_grad = times_transposed(grad_rows, down_weight[0])
    gate_grad_full, up_grad_full = swiglu_pull(act_grad)
    gate_grad = gate_grad_full.astype(jnp.bfloat16)
    up_grad = up_grad_full.astype(jnp.bfloat16)
    gate_bias_grad = jnp.sum(gate_grad.astype(jnp.float32), axis=0)
    up_bias_grad = jnp.sum(up_grad.astype(jnp.float32), axis=0)
    gate_weight_grad = inner_rows(expert_rows, gate_grad)
    up_weight_grad = inner_rows(expert_rows, up_grad)
    rows_grad = gradients_back(gate_grad, up_grad, gate_weight[0], up_weight[0], experts, capacity)
    normed_moe_grad = jnp.einsum(
        "ts,sd->td",
        dispatch.astype(jnp.float32),
        rows_grad.reshape(experts * capacity, width),
        precision=highest,
    )
    hidden_norm_grad, moe_gain_grad = moe_norm_pull(normed_moe_grad)
    hidden_grad = upstream + hidden_norm_grad
    attn_out_grad = hidden_grad.astype(jnp.bfloat16)
    output_bias_grad = jnp.sum(attn_out_grad.astype(jnp.float32), axis=0)
    full_query, full_key, full_value, full_output = (
        lax.all_gather(query_weight, ("seq", "exp", "dp"), axis=1, tiled=True),
        lax.all_gather(key_weight, ("seq", "exp", "dp"), axis=1, tiled=True),
        lax.all_gather(value_weight, ("seq", "exp", "dp"), axis=1, tiled=True),
        lax.all_gather(output_weight, ("seq", "exp", "dp"), axis=0, tiled=True),
    )
    mixed_grad = (
        times_transposed(attn_out_grad, full_output)
        .astype(jnp.bfloat16)
        .reshape(count_rows, kv_count, group, HD)
    )
    scores = score_block()
    probs = jnp.exp(scores - log_total[..., None])
    prob_grad = jnp.einsum(
        "qkgd,skd->kgqs", mixed_grad, all_values, preferred_element_type=jnp.float32
    )
    delta = jnp.sum(probs * prob_grad, axis=-1)
    score_grad = (probs * (prob_grad - delta[..., None])).astype(jnp.bfloat16)
    sink_grad = -jnp.sum(jnp.exp(sink_grid - log_total) * delta, axis=-1).reshape(head_count)
    value_grad = jnp.einsum(
        "kgqs,qkgd->skd", probs.astype(jnp.bfloat16), mixed_grad, preferred_element_type=jnp.float32
    )
    key_grad = (
        jnp.einsum("kgqs,qkgd->skd", score_grad, query_group, preferred_element_type=jnp.float32)
        * scale
    )
    query_grad = (
        jnp.einsum("kgqs,skd->qkgd", score_grad, all_keys, preferred_element_type=jnp.float32)
        * scale
    )
    key_share, value_share = (
        lax.psum_scatter(
            key_grad.reshape(seq_len, kv_count * HD), "seq", scatter_dimension=0, tiled=True
        ),
        lax.psum_scatter(
            value_grad.reshape(seq_len, kv_count * HD), "seq", scatter_dimension=0, tiled=True
        ),
    )
    query_lin_grad = (
        rotate(query_grad.reshape(count_rows, head_count, HD), cosine, -sine)
        .reshape(count_rows, head_count * HD)
        .astype(jnp.bfloat16)
    )
    key_lin_grad = (
        rotate(key_share.reshape(count_rows, kv_count, HD), cosine, -sine)
        .reshape(count_rows, kv_count * HD)
        .astype(jnp.bfloat16)
    )
    value_lin_grad = value_share.astype(jnp.bfloat16)
    query_bias_grad = jnp.sum(query_lin_grad.astype(jnp.float32), axis=0)
    key_bias_grad = jnp.sum(key_lin_grad.astype(jnp.float32), axis=0)
    value_bias_grad = jnp.sum(value_lin_grad.astype(jnp.float32), axis=0)
    normed_grad = (
        times_transposed(query_lin_grad, full_query)
        + times_transposed(key_lin_grad, full_key)
        + times_transposed(value_lin_grad, full_value)
    )
    resid_norm_grad, attn_gain_grad = attn_norm_pull(normed_grad)
    input_grad = hidden_grad + resid_norm_grad
    query_weight_grad = inner_rows(normed, query_lin_grad)
    key_weight_grad = inner_rows(normed, key_lin_grad)
    value_weight_grad = inner_rows(normed, value_lin_grad)
    output_weight_grad = inner_rows(mixed, attn_out_grad)
    query_owned, key_owned, value_owned, output_owned = (
        lax.psum_scatter(query_weight_grad, ("seq", "exp", "dp"), scatter_dimension=1, tiled=True),
        lax.psum_scatter(key_weight_grad, ("seq", "exp", "dp"), scatter_dimension=1, tiled=True),
        lax.psum_scatter(value_weight_grad, ("seq", "exp", "dp"), scatter_dimension=1, tiled=True),
        lax.psum_scatter(output_weight_grad, ("seq", "exp", "dp"), scatter_dimension=0, tiled=True),
    )
    summed = lax.psum(
        (
            attn_gain_grad,
            query_bias_grad,
            key_bias_grad,
            value_bias_grad,
            output_bias_grad,
            sink_grad,
            moe_gain_grad,
        ),
        ("seq", "exp", "dp"),
    )
    return (
        output[None],
        input_grad[None],
        summed[0],
        query_owned,
        summed[1],
        key_owned,
        summed[2],
        value_owned,
        summed[3],
        output_owned,
        summed[4],
        summed[5],
        summed[6],
        gate_weight_grad[None],
        gate_bias_grad[None],
        up_weight_grad[None],
        up_bias_grad[None],
        down_weight_grad[None],
        down_bias_grad[None],
    )

MESH = pl.DeviceIdType.MESH
HERE = (0, 0, 0)
SIBLING = (0, 1, 0)
ACROSS = (1, 0, 0)
ALONG = (0, 0, 1)
NEAR = (0, 2, 0)
FAR = (0, 4, 0)
ENDS = (0, 6, 0)
THIRD = (0, 8, 0)
FOURTH = (0, 16, 0)


def flip(place, mask):
    x, e, y = place
    if mask[0]:
        x = 1 - x
    if mask[2]:
        y = 1 - y
    if mask[1] & 8:
        e = 2 * (2 - lax.div(e, 4)) + lax.rem(e, 2)
    if mask[1] & 16:
        e = 2 * (3 - 3 * lax.div(e, 4)) + lax.rem(e, 2)
    step = 0
    for bit in (1, 2, 4):
        if mask[1] & bit:
            step = step + bit - 2 * bit * lax.rem(lax.div(e, bit), 2)
    return x, e + step, y


def both(left, right):
    return tuple(a ^ b for a, b in zip(left, right))


def place_here():
    return lax.axis_index("seq"), lax.axis_index("exp"), lax.axis_index("dp")


def block_of_all(place):
    x, e, y = place
    return (e * 2 + x) * 2 + y


def block_of_tokens(place):
    x, e, y = place
    return lax.rem(lax.div(e, 2), 2) * 2 + x


def block_of_heads(place):
    x, e, y = place
    return (lax.div(e, 4) * 2 + lax.rem(e, 2)) * 2 + y


GROUPS = {
    "all": (block_of_all, 32, SIBLING, ACROSS, ALONG, (NEAR, ENDS), 0.5),
    "tokens": (block_of_tokens, 4, None, ACROSS, NEAR, (), 0.5),
    "heads": (block_of_heads, 8, SIBLING, FAR, ALONG, (), 1.0),
}


def partners(group):
    _, _, sibling, first, second, line, _ = GROUPS[group]
    return ([sibling] if sibling else []) + [first, second] + list(line)


def copies(group):
    _, _, sibling, _, _, line, _ = GROUPS[group]
    if line:
        return 4 * 8 + 5
    return 8 if sibling else 4


class Sender:
    def __init__(self, place, send, recv):
        self.place, self.send, self.recv, self.started = place, send, recv, []
        self.maybe = []
        line_place = lax.div(place[1], 2)
        self.inner = (line_place == 1) | (line_place == 2)

    def plan(self, source, target, mask, lands=None):
        number = len(self.started) + len(self.maybe)
        return pltpu.make_async_remote_copy(
            src_ref=source,
            dst_ref=target,
            send_sem=self.send.at[number],
            recv_sem=self.recv.at[number if lands is None else lands],
            device_id=flip(self.place, mask),
            device_id_type=MESH,
        )

    def push(self, source, target, mask):
        copy = self.plan(source, target, mask)
        copy.start()
        self.started.append(copy)
        return copy

    def push_within(self, source, target, mask, lands=None, inner=True):
        copy = self.plan(source, target, mask, lands)
        number = len(self.started) + len(self.maybe)
        here = self.inner if inner else jnp.logical_not(self.inner)
        self.maybe.append((here, copy))
        pl.when(here)(copy.start)
        return copy, number

    def finish(self):
        for copy in self.started:
            copy.wait_send()
        for here, copy in self.maybe:
            pl.when(here)(copy.wait_send)


class Gather:
    def __init__(self, group, place, source, result, send, recv, local, share=None):
        self.index, _, self.sibling, self.first, self.second, line, usual = GROUPS[group]
        self.place, self.source, self.result = place, source, result
        self.rows = source.shape[0]
        share = usual if share is None else share
        self.cut = int(self.rows * share) // 16 * 16
        self.out = Sender(place, send, recv)
        self.own = pltpu.make_async_copy(source, self.at(HERE), local.at[0])
        self.masks = [HERE, NEAR, THIRD, FOURTH] if line else [HERE]
        self.ways, self.halves, self.lands, self.relayed = {}, {}, {}, []
        self.tails = {step: [] for step in range(len(self.masks))}

    def at(self, mask):
        return self.result.at[self.index(flip(self.place, mask))]

    def start(self):
        self.own.start()
        if len(self.masks) > 1:
            self.begin_line()

    def begin_line(self):
        self.near = self.out.push(self.source, self.at(HERE), NEAR)
        self.third, self.lands[2] = self.out.push_within(self.source, self.at(HERE), ENDS)

    def relay(self, step):
        if step in self.relayed:
            return
        self.relayed.append(step)
        if step == 1:
            self.near.wait_recv()
            self.fourth, self.lands[3] = self.out.push_within(self.at(NEAR), self.at(NEAR), ENDS)
            return
        copy = self.third if step == 2 else self.fourth
        pl.when(self.out.inner)(copy.wait_recv)
        block = self.at(self.masks[step])
        self.out.push_within(block, block, NEAR, self.lands[step])

    def reached(self, step):
        self.relay(step)
        if step > 1:
            copy = self.third if step == 2 else self.fourth
            pl.when(jnp.logical_not(self.out.inner))(copy.wait_recv)

    def pass_on(self, step, block, place):
        if self.sibling:
            self.tails[step].append(self.out.push(block, place, self.sibling))

    def plane(self, step):
        mask = self.masks[step]
        if step:
            self.reached(step)
        block = self.at(mask) if step else self.source
        self.ways[step] = (
            self.out.push(block, self.at(mask), self.first),
            self.out.push(block, self.at(mask), self.second),
        )
        self.pass_on(step, block, self.at(mask))

    def turn(self, step):
        halves = []
        mask, cut = self.masks[step], self.cut
        self.ways[step][0].wait_recv()
        seen = self.at(both(mask, self.first))
        if cut:
            halves.append(self.out.push(seen.at[:cut], seen.at[:cut], self.second))
        self.pass_on(step, seen, seen)
        self.ways[step][1].wait_recv()
        seen = self.at(both(mask, self.second))
        if cut < self.rows:
            halves.append(self.out.push(seen.at[cut:], seen.at[cut:], self.first))
        self.pass_on(step, seen, seen)
        self.halves[step] = halves

    def close(self, step):
        for half in self.halves[step]:
            half.wait_recv()
        seen = self.at(both(self.masks[step], both(self.first, self.second)))
        self.pass_on(step, seen, seen)

    def hop(self, number):
        for step in range(len(self.masks)):
            (self.plane, self.turn, self.close)[number](step)

    def passed(self, step):
        for copy in self.tails[step]:
            copy.wait_recv()

    def arrived(self):
        for step in range(len(self.masks)):
            self.passed(step)
        self.own.wait()

    def finish(self):
        self.out.finish()


def total(parts, low, high, store):
    def body(step, carry):
        rows = pl.ds(pl.multiple_of(low + step * 16, 16), 16)
        value = parts[0][rows].astype(jnp.float32)
        for part in parts[1:]:
            value = value + part[rows].astype(jnp.float32)
        store[rows] = value.astype(store.dtype)
        return carry

    if high > low:
        lax.fori_loop(0, (high - low) // 16, body, 0)


def by_tiles(width, tile, parts=2):
    size = -(-width // (128 * parts)) * 128
    for low in range(0, width, size):
        tile(low, min(size, width - low))


def seat_hot(seats, capacity, kind):
    lines = lax.broadcasted_iota(jnp.int32, (2 * capacity, seats.shape[-1]), 0)
    return (lines == seats).astype(kind)


def expert_sums(kind, rows, weights, seats, extra, collective, name, products=()):
    experts, pairs = seats.shape[1], seats.shape[2]
    thick = seats.shape[4]
    tokens = seats.shape[4] // 2
    half_rows = rows[0].shape[0] // experts
    pair_rows = half_rows // pairs
    capacity = pair_rows // 2
    hidden = rows[0].shape[1]
    width = weights[0].shape[1]
    first, second = ACROSS, ALONG
    masks = [FOURTH, THIRD, NEAR, HERE]
    rounds = len(masks)
    cut = tokens // 2
    count_rows, count_extra = len(rows), len(extra)
    copies_out = rounds * (pairs + 4) + 5

    def body(*refs):
        refs = list(refs)
        left = refs[:count_rows]
        stored = refs[count_rows : 2 * count_rows]
        seat_ref = refs[2 * count_rows]
        more = refs[2 * count_rows + 1 : 2 * count_rows + 1 + count_extra]
        rest = refs[2 * count_rows + 1 + count_extra :]
        thin_wide, rest = rest[: 2 * len(products)], rest[2 * len(products) :]
        result, rest = rest[0], rest[1:]
        made, rest = rest[: len(products)], rest[len(products) :]
        wide, rest = rest[:count_rows], rest[count_rows:]
        staged, away, joined, own, side, arrive, ends, send, recv, local, weight_sem = rest[:11]
        if products:
            thin_stage, wide_stage, gross, product_sem, made_sem = rest[11:]
        weight_copies = [
            pltpu.make_async_copy(stored[item], wide[item], weight_sem.at[item])
            for item in range(count_rows)
        ]
        for copy in weight_copies:
            copy.start()
        place = place_here()
        x, e, y = place
        greet = [SIBLING, first, second, NEAR, FAR, ENDS]
        barrier = pltpu.get_barrier_semaphore()
        for mask in greet:
            pl.semaphore_signal(barrier, inc=1, device_id=flip(place, mask), device_id_type=MESH)
        pl.semaphore_wait(barrier, len(greet))
        out = Sender(place, send, recv)

        def block(mask):
            there = flip(place, mask)
            return there[0] * 2 + there[2]

        halves = []
        for mask in masks:
            halves.append((flip(place, both(mask, SIBLING))[1], True))
            halves.append((flip(place, mask)[1], False))
        loads = {}

        def load(number):
            if number < len(halves):
                begin = pl.multiple_of(halves[number][0] * half_rows, 16)
                for item in range(count_rows):
                    copy = pltpu.make_async_copy(
                        left[item].at[pl.ds(begin, half_rows)],
                        staged.at[number % 2, item],
                        local.at[number % 2, item],
                    )
                    copy.start()
                    loads[number, item] = copy

        def make(number, store):
            load(number + 1)
            for item in range(count_rows):
                loads[number, item].wait()
                if number == 0:
                    weight_copies[item].wait()
            values = [staged[number % 2, item] for item in range(count_rows)]
            if kind == "result":
                part = halves[number][0]
                factors = []
                for pair in range(pairs):
                    hot = seat_hot(seat_ref[0, part, pair], capacity, jnp.float32)
                    factors.append(jnp.sum(hot * more[0][part, pair], axis=1, keepdims=True))
                factor = jnp.concatenate(factors, axis=0)
                once = jnp.where((x == 0) & (y == 0), 1.0, 0.0).astype(jnp.float32)

            def tile(low, size):
                area = pl.ds(low, size)
                value = jnp.dot(values[0], wide[0][:, area], preferred_element_type=jnp.float32)
                if kind == "gradient":
                    value += jnp.dot(values[1], wide[1][:, area], preferred_element_type=jnp.float32)
                else:
                    value = (value + once * more[1][:, area]) * factor
                store(low, size, value.astype(jnp.bfloat16))

            by_tiles(width, tile)

        def to_sibling(step):
            slot = step % 2

            def store(low, size, value):
                away[slot, :, pl.ds(low, size)] = value

            if step >= 2:
                for copy in sent[step - 2]:
                    copy.wait_send()
            make(2 * step, store)
            sent[step] = [
                out.push(
                    away.at[slot].at[pair * pair_rows : (pair + 1) * pair_rows],
                    joined.at[step, pair].at[pair_rows : 2 * pair_rows],
                    SIBLING,
                )
                for pair in range(pairs)
            ]

        def to_here(step):
            def store(low, size, value):
                for pair in range(pairs):
                    joined[step, pair, :pair_rows, pl.ds(low, size)] = value[
                        pair * pair_rows : (pair + 1) * pair_rows
                    ]

            make(2 * step + 1, store)

        def combine(step):
            for copy in sent[step]:
                copy.wait_recv()
            part = halves[2 * step + 1][0]
            for pair in range(pairs):
                hot = jnp.concatenate(
                    [seat_hot(seat_ref[mate, part, pair], capacity, jnp.bfloat16) for mate in range(2)],
                    axis=0,
                )

                def tile(low, size):
                    value = inner_rows(hot, joined[step, pair, :, pl.ds(low, size)])
                    value = value.astype(jnp.bfloat16)
                    own[step * 4 + pair * 2, :, pl.ds(low, size)] = value[:tokens]
                    own[step * 4 + pair * 2 + 1, :, pl.ds(low, size)] = value[tokens:]

                by_tiles(width, tile)

        def outward(step):
            corner = own.at[step * 4 + block(both(first, second))]
            return [
                out.push(corner.at[:cut], side.at[step].at[:cut], first),
                out.push(corner.at[cut:], side.at[step].at[cut:], second),
            ]

        def inward(step, parts):
            by_first = own.at[step * 4 + block(first)]
            by_second = own.at[step * 4 + block(second)]
            for part in parts:
                part.wait_recv()
            total([by_second, side.at[step]], 0, cut, by_second)
            total([by_first, side.at[step]], cut, tokens, by_first)
            return (
                out.push(by_first, arrive.at[step * 2], first),
                out.push(by_second, arrive.at[step * 2 + 1], second),
            )

        def close(step, ways):
            kept = own.at[step * 4 + block(HERE)]
            for way in ways:
                way.wait_recv()
            parts = [kept, arrive.at[step * 2], arrive.at[step * 2 + 1]]
            if masks[step] in (FOURTH, THIRD):
                total(parts, 0, tokens, kept)
                shared[step], _ = out.push_within(kept, ends.at[1 + step], NEAR, inner=False)
                return
            if masks[step] == NEAR:
                total(parts, 0, tokens, kept)
                reach.append((out.push(kept, ends.at[3], NEAR), None))
                return
            for copy, _ in reach:
                copy.wait_recv()
            parts += [ends.at[0], ends.at[3]]
            total(parts, 0, tokens, result)

        def across(step):
            kept = own.at[step * 4 + block(HERE)]

            @pl.when(out.inner)
            def _():
                shared[step].wait_recv()
                total([kept, ends.at[1 + step]], 0, tokens, kept)

            copy, number = out.push_within(kept, ends.at[0], masks[step], lands=reach[0][1] if reach else None)
            if not reach:
                reach.append((copy, number))

        chunks = rows[0].shape[0] // thick

        def product_loads(item, number):
            slot = lax.rem(number, 2)
            begin = pl.multiple_of(number * thick, 16)
            return [
                pltpu.make_async_copy(
                    thin_wide[2 * item + part].at[pl.ds(begin, thick)], stage.at[slot], product_sem.at[slot, part]
                )
                for part, stage in enumerate((thin_stage, wide_stage))
            ]

        written = []

        def multiply(item, begin, end):
            if begin == 0:
                for copy in product_loads(item, 0):
                    copy.start()
                if written:
                    written[-1].wait()
                else:
                    gross[...] = jnp.zeros_like(gross)

            def step(number, carry):
                @pl.when(number + 1 < chunks)
                def _():
                    for copy in product_loads(item, number + 1):
                        copy.start()

                for copy in product_loads(item, number):
                    copy.wait()
                slot = lax.rem(number, 2)
                keep = jnp.where(number == 0, 0.0, 1.0).astype(jnp.float32)

                def tile(low, size):
                    area = pl.ds(low, size)
                    value = inner_rows(thin_stage[slot], wide_stage[slot, :, area])
                    gross[:, area] = gross[:, area] * keep + value

                by_tiles(width, tile, 3)
                return carry

            lax.fori_loop(begin, end, step, 0)
            if end == chunks:
                copy = pltpu.make_async_copy(gross, made[item], made_sem.at[0])
                copy.start()
                written.append(copy)

        todo = [(item, begin) for item in range(len(products)) for begin in range(0, chunks, 3)]

        def some(number):
            for item, begin in todo[:number]:
                multiply(item, begin, min(begin + 3, chunks))
            del todo[:number]

        sent, corners, ways, reach, shared = {}, {}, {}, [], {}
        load(0)
        for step in range(rounds + 2):
            if step < rounds:
                to_sibling(step)
                to_here(step)
                combine(step)
                corners[step] = outward(step)
            if 0 <= step - 1 < rounds:
                ways[step - 1] = inward(step - 1, corners[step - 1])
            if step - 3 in (0, 1):
                across(step - 3)
            if 0 <= step - 2 < rounds:
                close(step - 2, ways[step - 2])
            some((2, 2, 3, 2, 0, 0)[step])
        some(len(todo))
        if written:
            written[-1].wait()
        for step in range(rounds):
            if step >= rounds - 2:
                for copy in sent[step]:
                    copy.wait_send()
        exchanged = {id(copy) for step in range(rounds) for copy in sent[step]}
        out.started = [copy for copy in out.started if id(copy) not in exchanged]
        out.finish()

    vmem, anywhere = pl.BlockSpec(memory_space=pltpu.VMEM), pl.BlockSpec(memory_space=pl.ANY)
    for_products = []
    if products:
        for_products = [
            pltpu.VMEM((2, thick, hidden), jnp.bfloat16),
            pltpu.VMEM((2, thick, width), jnp.bfloat16),
            pltpu.VMEM((hidden, width), jnp.float32),
            pltpu.SemaphoreType.DMA((2, 2)),
            pltpu.SemaphoreType.DMA((1,)),
        ]
    return pl.pallas_call(
        body,
        out_shape=[jax.ShapeDtypeStruct((tokens, width), jnp.float32)]
        + [jax.ShapeDtypeStruct((hidden, width), jnp.float32)] * len(products),
        in_specs=[anywhere] * (2 * count_rows)
        + [vmem] * (1 + count_extra)
        + [anywhere] * (2 * len(products)),
        out_specs=[vmem] + [anywhere] * len(products),
        scratch_shapes=[pltpu.VMEM(weight.shape, jnp.bfloat16) for weight in weights]
        + [
            pltpu.VMEM((2, count_rows, half_rows, hidden), jnp.bfloat16),
            pltpu.VMEM((2, half_rows, width), jnp.bfloat16),
            pltpu.VMEM((rounds, pairs, 2 * pair_rows, width), jnp.bfloat16),
            pltpu.VMEM((rounds * 4, tokens, width), jnp.bfloat16),
            pltpu.VMEM((rounds, tokens, width), jnp.bfloat16),
            pltpu.VMEM((rounds * 2, tokens, width), jnp.bfloat16),
            pltpu.VMEM((4, tokens, width), jnp.bfloat16),
            pltpu.SemaphoreType.DMA((copies_out,)),
            pltpu.SemaphoreType.DMA((copies_out,)),
            pltpu.SemaphoreType.DMA((2, count_rows)),
            pltpu.SemaphoreType.DMA((count_rows,)),
        ]
        + for_products,
        compiler_params=pltpu.CompilerParams(
            collective_id=collective, has_side_effects=True, vmem_limit_bytes=62 * 1024 * 1024
        ),
        name=name,
    )(*rows, *weights, seats, *extra, *[array for pair in products for array in pair])


def expert_rows_kernel(own_block, cotangents, weights, biases, seats, shares, capacity, collective, name):
    experts, pairs = seats.shape[0], seats.shape[1]
    tokens, width = own_block.shape
    blocks = cotangents.shape[0]
    hidden = weights[0].shape[0]
    pair_rows = 2 * capacity
    half_rows = pairs * pair_rows
    row_count = experts * half_rows
    copies_out = copies("all")

    def body(*refs):
        (own_ref, cot_ref, *stored, gate_bias, up_bias, seat_ref, share_ref) = refs[:9]
        (rows_out, grads_out, act_out, dgate_out, dup_out, gate_sum, up_sum, down_sum, held) = refs[9:18]
        (stage, lines, thin, pre, back, gate, up, down) = refs[18:26]
        (send, recv, local, load_sem, line_sem, thin_sem, weight_sem) = refs[26:]
        weight_copies = [
            pltpu.make_async_copy(stored[item], goal, weight_sem.at[item])
            for item, goal in enumerate((gate, up, down))
        ]
        for copy in weight_copies[::-1]:
            copy.start()
        place = place_here()
        x, e, y = place
        greet = partners("all")
        barrier = pltpu.get_barrier_semaphore()
        for mask in greet:
            pl.semaphore_signal(barrier, inc=1, device_id=flip(place, mask), device_id_type=MESH)
        pl.semaphore_wait(barrier, len(greet))
        work = Gather("all", place, own_ref, held, send, recv, local)
        work.start()
        gate_sum[...] = jnp.zeros_like(gate_sum)
        up_sum[...] = jnp.zeros_like(up_sum)
        down_sum[...] = jnp.zeros_like(down_sum)
        halves = []
        for mask in work.masks:
            halves.append(flip(place, mask)[1])
            halves.append(flip(place, both(mask, SIBLING))[1])
        turnstile = {"load": 0, "line": 0}
        line_copies, thin_copies = [], []

        fetched = {}

        def fetch(scaled, number):
            bank = len(fetched) % 2
            begin = halves[number] * pairs * 2
            copies_in = [
                pltpu.make_async_copy(
                    (cot_ref if scaled else held).at[pl.ds(begin + 2 * pair, 2)],
                    stage.at[2 * bank + pair],
                    load_sem.at[2 * bank + pair],
                )
                for pair in range(pairs)
            ]
            for copy in copies_in:
                copy.start()
            fetched[scaled, number] = (bank, copies_in)

        def pick(scaled, number):
            part = halves[number]
            bank, copies_in = fetched[scaled, number]
            slot = turnstile["line"] % 2
            turnstile["line"] += 1
            if len(line_copies) >= 2:
                line_copies[-2].wait()
            for pair in range(pairs):
                copies_in[pair].wait()
                hot = seat_hot(seat_ref[part, pair], capacity, jnp.float32)
                if scaled:
                    factor = jnp.sum(hot * share_ref[part, pair], axis=1, keepdims=True)
                hot = hot.astype(jnp.bfloat16)
                blocks_here = stage[2 * bank + pair].reshape(2 * tokens, width)
                value = jnp.dot(hot, blocks_here, preferred_element_type=jnp.float32)
                if scaled:
                    value = value * factor
                value = value.astype(jnp.bfloat16)
                lines[slot, pair * pair_rows : (pair + 1) * pair_rows] = value
                if scaled:
                    down_sum[...] += jnp.sum(value.astype(jnp.float32), axis=0, keepdims=True)
            copy = pltpu.make_async_copy(
                lines.at[slot],
                (grads_out if scaled else rows_out).at[
                    pl.ds(pl.multiple_of(part * half_rows, 16), half_rows)
                ],
                line_sem.at[slot],
            )
            copy.start()
            line_copies.append(copy)
            return lines.at[slot]

        def backward(number):
            picked = pick(True, number)
            if number == 0:
                weight_copies[2].wait()
            back[number] = times_transposed(picked[...], down[...])

        def forward(number):
            part = halves[number]
            picked = pick(False, number)
            if number == 0:
                weight_copies[0].wait()
                weight_copies[1].wait()
            pre[0] = times_transposed(picked[...], gate[...])
            pre[1] = times_transposed(picked[...], up[...])
            slot = number % 2
            if number >= 2:
                for copy in thin_copies[-6:-3]:
                    copy.wait()

            def chunk(step, sums):
                area = pl.ds(pl.multiple_of(step * 16, 16), 16)
                gate_tanh = jnp.tanh((pre[0, area] + gate_bias[...]) * (1.0 / clip_level))
                up_tanh = jnp.tanh((pre[1, area] + up_bias[...]) * (1.0 / clip_level))
                gate_soft = clip_level * gate_tanh
                up_more = clip_level * up_tanh + 1.0
                bend = jax.nn.sigmoid(glu_alpha * gate_soft)
                glow = gate_soft * bend
                grad = back[number, area]
                dgate = grad * up_more * (bend + glu_alpha * glow * (1.0 - bend))
                dgate = (dgate * (1.0 - gate_tanh * gate_tanh)).astype(jnp.bfloat16)
                dup = (grad * glow * (1.0 - up_tanh * up_tanh)).astype(jnp.bfloat16)
                thin[slot, 0, area] = (glow * up_more).astype(jnp.bfloat16)
                thin[slot, 1, area] = dgate
                thin[slot, 2, area] = dup
                return sums[0] + dgate.astype(jnp.float32), sums[1] + dup.astype(jnp.float32)

            zero = jnp.zeros((16, hidden), jnp.float32)
            sums = lax.fori_loop(0, half_rows // 16, chunk, (zero, zero))
            gate_sum[...] += jnp.sum(sums[0], axis=0, keepdims=True)
            up_sum[...] += jnp.sum(sums[1], axis=0, keepdims=True)
            for item, goal in enumerate((act_out, dgate_out, dup_out)):
                copy = pltpu.make_async_copy(
                    thin.at[slot, item],
                    goal.at[pl.ds(pl.multiple_of(part * half_rows, 16), half_rows)],
                    thin_sem.at[slot, item],
                )
                copy.start()
                thin_copies.append(copy)

        order = ["p0B0B1b0B2b1t0p1r2B3b2c0o0F0b3r3p2t1w0F1f0B4f1c1F2b4"]
        order += ["p3t2w1F3f2B5f3B6b5c2F4b6w2F5f4t3B7f5b7c3F6w3F7f6f7"]
        acts = {
            "p": work.plane,
            "t": work.turn,
            "c": work.close,
            "w": work.passed,
            "r": work.relay,
            "o": lambda number: work.own.wait(),
            "B": lambda number: fetch(True, number),
            "F": lambda number: fetch(False, number),
            "b": backward,
            "f": forward,
        }
        order = "".join(order)
        for low in range(0, len(order), 2):
            acts[order[low]](int(order[low + 1]))
        for copy in line_copies[-2:] + thin_copies[-6:]:
            copy.wait()
        work.finish()

    vmem, anywhere = pl.BlockSpec(memory_space=pltpu.VMEM), pl.BlockSpec(memory_space=pl.ANY)
    bf16, f32 = jnp.bfloat16, jnp.float32
    return pl.pallas_call(
        body,
        out_shape=[
            jax.ShapeDtypeStruct((row_count, width), bf16),
            jax.ShapeDtypeStruct((row_count, width), bf16),
            jax.ShapeDtypeStruct((row_count, hidden), bf16),
            jax.ShapeDtypeStruct((row_count, hidden), bf16),
            jax.ShapeDtypeStruct((row_count, hidden), bf16),
            jax.ShapeDtypeStruct((1, hidden), f32),
            jax.ShapeDtypeStruct((1, hidden), f32),
            jax.ShapeDtypeStruct((1, width), f32),
            jax.ShapeDtypeStruct((blocks, tokens, width), bf16),
        ],
        in_specs=[anywhere] * 5 + [vmem] * 4,
        out_specs=[anywhere] * 5 + [vmem] * 3 + [anywhere],
        scratch_shapes=[
            pltpu.VMEM((4, 2, tokens, width), bf16),
            pltpu.VMEM((2, half_rows, width), bf16),
            pltpu.VMEM((2, 3, half_rows, hidden), bf16),
            pltpu.VMEM((2, half_rows, hidden), f32),
            pltpu.VMEM((experts, half_rows, hidden), f32),
        ]
        + [pltpu.VMEM(weight.shape, bf16) for weight in weights]
        + [
            pltpu.SemaphoreType.DMA((copies_out,)),
            pltpu.SemaphoreType.DMA((copies_out,)),
            pltpu.SemaphoreType.DMA((1,)),
            pltpu.SemaphoreType.DMA((4,)),
            pltpu.SemaphoreType.DMA((2,)),
            pltpu.SemaphoreType.DMA((2, 3)),
            pltpu.SemaphoreType.DMA((3,)),
        ],
        compiler_params=pltpu.CompilerParams(
            collective_id=collective, has_side_effects=True, vmem_limit_bytes=60 * 1024 * 1024
        ),
        name=name,
    )(own_block, cotangents, *weights, *biases, seats, shares)


class Scatter:
    def __init__(self, group, place, source, result, side, arrive, send, recv, spare, mate=None):
        self.index, _, self.sibling, self.first, self.second, _, share = GROUPS[group]
        self.place, self.source, self.result = place, source, result
        self.side, self.arrive, self.mate = side, arrive, mate
        self.rows = result.shape[0]
        self.cut = int(self.rows * (1.0 - share)) // 16 * 16
        self.corner = both(self.first, self.second)
        self.out = Sender(place, send, recv)
        self.crossing = {}

    def at(self, mask):
        return self.source.at[self.index(flip(self.place, mask))]

    def cross(self):
        for spot, mask in enumerate((self.corner, self.first, self.second, HERE)):
            self.crossing[mask] = (
                self.out.push(self.at(both(mask, self.sibling)), self.mate.at[spot], self.sibling),
                self.mate.at[spot],
            )

    def ready(self, mask):
        if not self.sibling:
            return [self.at(mask)]
        copy, block = self.crossing[mask]
        copy.wait_recv()
        return [self.at(mask), block]

    def outward(self):
        corner, cut = self.at(self.corner), self.cut
        parts = self.ready(self.corner)
        if len(parts) > 1:
            total(parts, 0, self.rows, corner)
        self.halves = []
        if cut:
            self.halves.append(self.out.push(corner.at[:cut], self.side.at[:cut], self.first))
        if cut < self.rows:
            self.halves.append(self.out.push(corner.at[cut:], self.side.at[cut:], self.second))

    def inward(self):
        by_first, by_second = self.ready(self.first), self.ready(self.second)
        for half in self.halves:
            half.wait_recv()
        cut, rows = self.cut, self.rows
        total(by_second + [self.side], 0, cut, by_second[0])
        total(by_first + [self.side], cut, rows, by_first[0])
        if self.sibling:
            total(by_second, cut, rows, by_second[0])
            total(by_first, 0, cut, by_first[0])
        self.ways = (
            self.out.push(by_first[0], self.arrive.at[0], self.first),
            self.out.push(by_second[0], self.arrive.at[1], self.second),
        )

    def close(self):
        parts = self.ready(HERE)
        for way in self.ways:
            way.wait_recv()
        total(parts + [self.arrive.at[0], self.arrive.at[1]], 0, self.rows, self.result)

    def finish(self):
        self.out.finish()


def lanes(shape):
    return lax.broadcasted_iota(jnp.int32, shape, len(shape) - 1)


def swapped(value):
    width = value.shape[-1]
    upper = pltpu.roll(value, width - HD // 2, len(value.shape) - 1)
    lower = pltpu.roll(value, HD // 2, len(value.shape) - 1)
    return jnp.where(lanes(value.shape) % HD < HD // 2, upper, lower)


def halves_of(value, member):
    low = lanes(value.shape) < HD
    zero = jnp.zeros_like(value)
    if member == 0:
        kept = jnp.where(low, value, zero)
        return kept, pltpu.roll(kept, HD, 1)
    kept = jnp.where(low, zero, value)
    return pltpu.roll(kept, HD, 1), kept


def seen(marks, held, first_key=0):
    rows = marks.shape[1]
    lines = []
    for query in range(2):
        parts = []
        for key in range(2):
            if key > query:
                parts.append(jnp.zeros((rows, rows), jnp.bool_))
                continue
            same = marks[held + query] == marks[held + key].T
            if key == query:
                down = lax.broadcasted_iota(jnp.int32, (rows, rows), 0)
                same = same & (down >= lanes((rows, rows)))
            parts.append(same)
        lines.append(parts)
    return lines


def mask_of(marks, held):
    lines = seen(marks, held)
    return jnp.concatenate(
        [
            jnp.concatenate([jnp.where(part, 1.0, 0.0) for part in parts], axis=1)
            for parts in lines
        ],
        axis=0,
    )


def pick_lane(value, number):
    return jnp.sum(jnp.where(lanes(value.shape) == number, value, 0.0), axis=1, keepdims=True)


def attention_forward(
    normed, query_rows, key_rows, value_rows, output_rows, marks, table, extra, biases, tables, sinks, collective, name
):
    tokens, width = normed.shape
    block = 4 * tokens
    seq_len = 2 * tokens
    columns = 8 * query_rows.shape[0]
    pairs = columns // 128
    scale = 1.0 / math.sqrt(HD)
    bf16, f32 = jnp.bfloat16, jnp.float32
    gathers = [
        ("tokens", normed),
        ("heads", query_rows),
        ("heads", key_rows),
        ("heads", value_rows),
        ("tokens", marks),
        ("heads", output_rows),
        ("all", table),
        ("all", extra),
    ]
    count = len(gathers)

    def body(*refs):
        refs = list(refs)

        def take(number):
            got = refs[:number]
            del refs[:number]
            return got

        sources = take(count)
        query_bias, key_bias, value_bias, cosine, sine, sink_ref = take(6)
        (result, query_out, key_out, value_out, mixed_out, lse_out, mask) = take(7)
        kept_out = take(5)
        far_out = take(2)
        held = take(count - 2)
        (key_half, value_half, partial, side, arrive) = take(5)
        sems = [take(3) for _ in range(count)]
        sum_sems = take(3)
        (keep_sem,) = take(1)
        place = place_here()
        greet = []
        for group, _ in gathers:
            greet += [step for step in partners(group) if step not in greet]
        barrier = pltpu.get_barrier_semaphore()
        for step in greet:
            pl.semaphore_signal(barrier, inc=1, device_id=flip(place, step), device_id_type=MESH)
        pl.semaphore_wait(barrier, len(greet))
        works = [
            Gather(
                group, place, sources[item], (held + far_out)[item], *sems[item], share=0.25 if item == 7 else None
            )
            for item, (group, _) in enumerate(gathers)
        ]
        all_tokens, all_query, all_key, all_value, all_marks, all_output = held
        early, output_work, table_work, extra_work = works[:5], works[5], works[6], works[7]
        early = [early[4]] + early[:4]
        table_work.start()
        for work in early:
            work.start()
            work.plane(0)
        extra_work.start()
        extra_work.plane(0)
        early[0].turn(0)
        table_work.relay(1)
        table_work.relay(2)
        for work in early[1:]:
            work.turn(0)
        extra_work.turn(0)
        extra_work.plane(1)
        extra_work.relay(2)
        output_work.start()
        output_work.plane(0)
        for work in early:
            work.close(0)
        for work in early:
            work.passed(0)
            work.own.wait()
        keeps = []

        def keep(item, goal):
            copy = pltpu.make_async_copy(held[item], kept_out[goal], keep_sem.at[goal])
            copy.start()
            keeps.append(copy)

        for item in range(4):
            keep(item, item)
        x_all = all_tokens[...].reshape(block, width)

        def turned(value, low):
            return value * cosine[...] + swapped(value) * sine[...]

        def project(number, carry):
            weight = all_query[pl.ds(pl.multiple_of(2 * number, 2), 2)].reshape(256, width)
            value = times_transposed(x_all, weight)
            for part in range(2):
                area = pl.ds(pl.multiple_of((2 * number + part) * 128, 128), 128)
                head = value[:, part * 128 : (part + 1) * 128] + query_bias[:, area]
                query_out[:, area] = turned(head, 0).astype(bf16)
            return carry

        lax.fori_loop(0, pairs // 2, project, 0)
        key = times_transposed(x_all, all_key[...].reshape(128, width)) + key_bias[...]
        key = turned(key, 0).astype(bf16)
        key_out[...] = key
        value = times_transposed(x_all, all_value[...].reshape(128, width)) + value_bias[...]
        value = value.astype(bf16)
        value_out[...] = value
        for member in range(2):
            for part, half in enumerate(halves_of(key, member)):
                key_half[2 * member + part] = half
            for part, half in enumerate(halves_of(value, member)):
                value_half[2 * member + part] = half
        for half in range(2):
            mask[half] = mask_of(all_marks, 2 * half)
        table_work.relay(3)
        extra_work.close(0)
        extra_work.relay(3)
        extra_work.plane(2)
        lse_out[...] = jnp.zeros_like(lse_out)

        def attend(number, carry):
            pair = lax.div(number, 2)
            half = lax.rem(number, 2)
            member = lax.div(pair, pairs // 2)
            rows = pl.ds(pl.multiple_of(half * seq_len, seq_len), seq_len)
            area = pl.ds(pl.multiple_of(pair * 128, 128), 128)
            query = query_out[rows, area]
            mixed = jnp.zeros((seq_len, 128), f32)
            for part in range(2):
                raw = times_transposed(query, key_half[2 * member + part, rows]) * scale
                raw = jnp.where(mask[half] > 0.0, raw, masked_score)
                sink = sink_ref[0, 2 * pair + part]
                peak = jnp.maximum(jnp.max(raw, axis=1, keepdims=True), sink)
                mass = jnp.sum(jnp.exp(raw - peak), axis=1, keepdims=True) + jnp.exp(sink - peak)
                lse = peak + jnp.log(mass)
                probs = jnp.exp(raw - lse).astype(bf16)
                mixed = mixed + jnp.dot(
                    probs, value_half[2 * member + part, rows], preferred_element_type=f32
                )
                spot = lanes((seq_len, 128)) == 2 * pair + part
                lse_out[rows] = jnp.where(spot, lse, lse_out[rows])
            mixed_out[rows, area] = mixed.astype(bf16)
            return carry

        lax.fori_loop(0, pairs, attend, 0)
        extra_work.turn(1)
        output_work.turn(0)
        lax.fori_loop(pairs, 2 * pairs, attend, 0)
        table_work.hop(0)
        extra_work.plane(3)
        output_work.close(0)
        output_work.passed(0)
        output_work.own.wait()
        keep(5, 4)

        def tile(low, size):
            weight = all_output[:, :, pl.ds(low, size)].reshape(columns, size)
            value = jnp.dot(mixed_out[...], weight, preferred_element_type=f32).astype(bf16)
            partial[:, :, pl.ds(low, size)] = value.reshape(4, tokens, size)

        by_tiles(width, tile)
        run = Scatter("tokens", place, partial, result, side, arrive, *sum_sems)
        run.outward()
        extra_work.close(1)
        extra_work.turn(2)
        run.inward()
        extra_work.close(2)
        table_work.hop(1)
        extra_work.turn(3)
        run.close()
        table_work.hop(2)
        extra_work.close(3)
        for work in (table_work, extra_work):
            work.arrived()
        run.finish()
        for copy in keeps:
            copy.wait()
        for work in works:
            work.finish()

    vmem, anywhere = pl.BlockSpec(memory_space=pltpu.VMEM), pl.BlockSpec(memory_space=pl.ANY)
    smem = pl.BlockSpec(memory_space=pltpu.SMEM)
    kept = [(4,) + normed.shape] + [(8,) + rows.shape for rows in (query_rows, key_rows, value_rows, output_rows)]
    blocks = [GROUPS[group][1] for group, _ in gathers]
    return pl.pallas_call(
        body,
        out_shape=[
            jax.ShapeDtypeStruct((tokens, width), f32),
            jax.ShapeDtypeStruct((block, columns), bf16),
            jax.ShapeDtypeStruct((block, 128), bf16),
            jax.ShapeDtypeStruct((block, 128), bf16),
            jax.ShapeDtypeStruct((block, columns), bf16),
            jax.ShapeDtypeStruct((block, 128), f32),
            jax.ShapeDtypeStruct((2, seq_len, seq_len), f32),
        ]
        + [jax.ShapeDtypeStruct(shape, bf16) for shape in kept]
        + [
            jax.ShapeDtypeStruct((blocks[item],) + array.shape, array.dtype)
            for item, (_, array) in list(enumerate(gathers))[-2:]
        ],
        in_specs=[anywhere] * count + [vmem] * 5 + [smem],
        out_specs=[vmem] * 7 + [anywhere] * 7,
        scratch_shapes=[
            pltpu.VMEM((blocks[item],) + array.shape, array.dtype)
            for item, (_, array) in enumerate(gathers[:-2])
        ]
        + [
            pltpu.VMEM((4, block, 128), bf16),
            pltpu.VMEM((4, block, 128), bf16),
            pltpu.VMEM((4, tokens, width), bf16),
            pltpu.VMEM((tokens, width), bf16),
            pltpu.VMEM((2, tokens, width), bf16),
        ]
        + [
            pltpu.SemaphoreType.DMA((size,))
            for group, _ in gathers
            for size in (copies(group), copies(group), 1)
        ]
        + [pltpu.SemaphoreType.DMA((copies("tokens"),))] * 2
        + [pltpu.SemaphoreType.DMA((1,)), pltpu.SemaphoreType.DMA((5,))],
        compiler_params=pltpu.CompilerParams(
            collective_id=collective, has_side_effects=True, vmem_limit_bytes=60 * 1024 * 1024
        ),
        name=name,
    )(*[array for _, array in gathers], *biases, *tables, sinks)


def attention_backward(
    outer, query, key, value, mixed, log_total, mask, tokens_kept, weights, tables, sinks, gain, small, collective, name
):
    tokens, width = outer.shape
    block = 4 * tokens
    seq_len = 2 * tokens
    columns = query.shape[1]
    pairs = columns // 128
    scale = 1.0 / math.sqrt(HD)
    bf16, f32 = jnp.bfloat16, jnp.float32
    owned = [rows.shape[1] for rows in weights]
    groups = ["heads"] * 4 + ["tokens"]

    def body(*refs):
        refs = list(refs)

        def take(number):
            got = refs[:number]
            del refs[:number]
            return got

        (outer_ref,) = take(1)
        query_ref, key_ref, value_ref, mixed_ref, lse_ref, mask_ref = take(6)
        stored = take(5)
        cosine, sine, sink_ref, gain_ref, small_ref = take(5)
        results = take(5)
        (small_out,) = take(1)
        held = take(5)
        grads, key_half, value_half = take(3)
        mixed_grad, query_grad, key_grad, value_grad = take(4)
        key_sum, value_sum, sink_sum, small_own, small_all = take(5)
        output_part, key_part, value_part = take(3)
        mates, sides, arrives = take(4), take(5), take(5)
        load_sem, gather_sems, small_sems = take(1)[0], take(3), take(3)
        sum_sems = [take(3) for _ in groups]
        place = place_here()
        greet = []
        for group in ("tokens", "heads", "all"):
            greet += [step for step in partners(group) if step not in greet]
        barrier = pltpu.get_barrier_semaphore()
        for step in greet:
            pl.semaphore_signal(barrier, inc=1, device_id=flip(place, step), device_id_type=MESH)
        pl.semaphore_wait(barrier, len(greet))
        work = Gather("tokens", place, outer_ref, grads, *gather_sems)
        work.start()
        work.plane(0)
        loads = []
        for item in (4, 1, 2, 3, 0):
            copy = pltpu.make_async_copy(stored[item], held[item], load_sem.at[item])
            copy.start()
            loads.append(copy)
        all_tokens, all_query, all_key, all_value, all_output = held
        for member in range(2):
            for part, half in enumerate(halves_of(key_ref[...], member)):
                key_half[2 * member + part] = half
            for part, half in enumerate(halves_of(value_ref[...], member)):
                value_half[2 * member + part] = half
        key_sum[...] = jnp.zeros_like(key_sum)
        value_sum[...] = jnp.zeros_like(value_sum)
        sink_sum[...] = jnp.zeros_like(sink_sum)
        small_own[...] = small_ref[...]
        work.turn(0)
        work.close(0)
        work.own.wait()
        work.finish()

        parts = [all_output, key_part, value_part, output_part, grads]
        sums = [
            Scatter(
                group,
                place,
                parts[item],
                results[item],
                sides[item],
                arrives[item],
                *sum_sems[item],
                mate=mates[item] if group == "heads" else None,
            )
            for item, group in enumerate(groups)
        ]
        of_query, of_key, of_value, of_output, of_tokens = sums

        def output_gradient(number, carry):
            area = pl.ds(pl.multiple_of(number * 128, 128), 128)
            rows = inner_rows(mixed_ref[:, area], grads[...].reshape(block, width))
            output_part[number] = rows.astype(bf16)
            return carry

        lax.fori_loop(0, pairs, output_gradient, 0)
        of_output.cross()
        loads[0].wait()

        def project(number, carry):
            weight = all_output[pl.ds(pl.multiple_of(2 * number, 2), 2)].reshape(256, width)
            area = pl.ds(pl.multiple_of(number * 256, 256), 256)
            mixed_grad[:, area] = times_transposed(
                grads[...].reshape(block, width), weight
            ).astype(bf16)
            return carry

        lax.fori_loop(0, pairs // 2, project, 0)
        of_output.outward()

        def back(value):
            return value * cosine[:seq_len] - swapped(value) * sine[:seq_len]

        def attend(number, carry):
            pair = lax.div(number, 2)
            half = lax.rem(number, 2)
            member = lax.div(pair, pairs // 2)
            rows = pl.ds(pl.multiple_of(half * seq_len, seq_len), seq_len)
            area = pl.ds(pl.multiple_of(pair * 128, 128), 128)
            queries = query_ref[rows, area]
            upstream = mixed_grad[rows, area]
            low = lanes((seq_len, 128)) < HD
            made = jnp.zeros((seq_len, 128), f32)
            for part in range(2):
                head = 2 * pair + part
                keys = key_half[2 * member + part, rows]
                lse = pick_lane(lse_ref[rows], head)
                raw = times_transposed(queries, keys) * scale
                raw = jnp.where(mask_ref[half] > 0.0, raw, masked_score)
                probs = jnp.exp(raw - lse)
                grad = times_transposed(upstream, value_half[2 * member + part, rows])
                delta = jnp.sum(probs * grad, axis=1, keepdims=True)
                inner = (probs * (grad - delta)).astype(bf16)
                made = made + jnp.dot(inner, keys, preferred_element_type=f32)
                mine = low if part == 0 else jnp.logical_not(low)
                value_sum[member, rows] += jnp.where(mine, inner_rows(probs.astype(bf16), upstream), 0.0)
                key_sum[member, rows] += jnp.where(mine, inner_rows(inner, queries), 0.0)
                lost = jnp.sum(jnp.exp(sink_ref[0, head] - lse) * delta, axis=0, keepdims=True)
                sink_sum[...] -= jnp.where(lanes((1, 128)) == head, lost, 0.0)
            query_grad[rows, area] = back(made * scale).astype(bf16)
            return carry

        lax.fori_loop(0, pairs, attend, 0)
        of_output.inward()
        lax.fori_loop(pairs, 2 * pairs, attend, 0)
        low = lanes((seq_len, 128)) < HD
        for half in range(2):
            rows = pl.ds(half * seq_len, seq_len)

            def joined(sums):
                first = sums[0, rows] + pltpu.roll(sums[0, rows], HD, 1)
                second = sums[1, rows] + pltpu.roll(sums[1, rows], HD, 1)
                return jnp.where(low, first, second)

            key_grad[rows] = back(joined(key_sum) * scale).astype(bf16)
            value_grad[rows] = joined(value_sum).astype(bf16)
        for copy in loads[1:]:
            copy.wait()

        def tile(low_column, size):
            area = pl.ds(low_column, size)

            def rows_of(weight):
                return weight[:, :, area].reshape(-1, size)

            total_grad = jnp.dot(query_grad[...], rows_of(all_query), preferred_element_type=f32)
            total_grad += jnp.dot(key_grad[...], rows_of(all_key), preferred_element_type=f32)
            total_grad += jnp.dot(value_grad[...], rows_of(all_value), preferred_element_type=f32)
            gained = total_grad * all_tokens[:, :, area].reshape(block, size).astype(f32)
            small_own[0:1, area] = jnp.sum(gained, axis=0, keepdims=True) / gain_ref[:, area]
            grads[:, :, area] = total_grad.astype(bf16).reshape(4, tokens, size)

        by_tiles(width, tile)
        low_column = 0
        for array in (query_grad, key_grad, value_grad):
            size = array.shape[1]
            small_own[3:4, low_column : low_column + size] = jnp.sum(
                array[...].astype(f32), axis=0, keepdims=True
            )
            low_column += size
        small_own[3:4, low_column : low_column + 128] = sink_sum[...]
        spread = Gather("all", place, small_own, small_all, *small_sems)
        spread.start()
        of_tokens.outward()

        def query_gradient(number, carry):
            area = pl.ds(pl.multiple_of(number * 128, 128), 128)
            rows = inner_rows(query_grad[:, area], all_tokens[...].reshape(block, width))
            all_output[number] = rows.astype(bf16)
            return carry

        lax.fori_loop(0, pairs, query_gradient, 0)
        of_query.cross()
        for goal, grad in ((key_part, key_grad), (value_part, value_grad)):
            rows = inner_rows(grad[...], all_tokens[...].reshape(block, width))
            goal[...] = rows.astype(bf16).reshape(goal.shape)
        of_key.cross()
        of_value.cross()
        spread.relay(1)
        spread.relay(2)
        of_query.outward()
        of_key.outward()
        of_value.outward()
        spread.relay(3)
        of_tokens.inward()
        spread.hop(0)
        of_query.inward()
        of_key.inward()
        of_value.inward()
        spread.hop(1)
        of_tokens.close()
        spread.hop(2)
        of_output.close()
        of_query.close()
        of_key.close()
        of_value.close()
        spread.arrived()
        spread.finish()
        blocks = small_all.shape[0]
        whole = small_all[0]
        for number in range(1, blocks):
            whole = whole + small_all[number]
        small_out[0:4] = whole[0:4]
        for near in range(2):
            for side in range(2):
                chosen = [
                    number for number in range(blocks) if (number // 8 % 2, number // 2 % 2) == (near, side)
                ]
                part = small_all[chosen[0], 3:4]
                for number in chosen[1:]:
                    part = part + small_all[number, 3:4]
                small_out[4 + 2 * near + side : 5 + 2 * near + side] = part
        for part in sums:
            part.finish()

    vmem, anywhere = pl.BlockSpec(memory_space=pltpu.VMEM), pl.BlockSpec(memory_space=pl.ANY)
    smem = pl.BlockSpec(memory_space=pltpu.SMEM)
    rows_of = owned + [tokens]
    kept = [tokens_kept] + list(weights)
    return pl.pallas_call(
        body,
        out_shape=[jax.ShapeDtypeStruct((rows, width), f32) for rows in rows_of]
        + [jax.ShapeDtypeStruct(small.shape, f32)],
        in_specs=[anywhere] + [vmem] * 6 + [anywhere] * 5 + [vmem] * 2 + [smem] + [vmem] * 2,
        out_specs=[vmem] * 6,
        scratch_shapes=[pltpu.VMEM(array.shape, bf16) for array in kept]
        + [
            pltpu.VMEM((4, tokens, width), bf16),
            pltpu.VMEM((4, block, 128), bf16),
            pltpu.VMEM((4, block, 128), bf16),
            pltpu.VMEM((block, columns), bf16),
            pltpu.VMEM((block, columns), bf16),
            pltpu.VMEM((block, 128), bf16),
            pltpu.VMEM((block, 128), bf16),
            pltpu.VMEM((2, block, 128), f32),
            pltpu.VMEM((2, block, 128), f32),
            pltpu.VMEM((1, 128), f32),
            pltpu.VMEM(small.shape, f32),
            pltpu.VMEM((GROUPS["all"][1],) + small.shape, f32),
            pltpu.VMEM(weights[3].shape, bf16),
            pltpu.VMEM(weights[1].shape, bf16),
            pltpu.VMEM(weights[2].shape, bf16),
        ]
        + [pltpu.VMEM((4, rows, width), bf16) for rows in owned]
        + [pltpu.VMEM((rows, width), bf16) for rows in rows_of]
        + [pltpu.VMEM((2, rows, width), bf16) for rows in rows_of]
        + [pltpu.SemaphoreType.DMA((5,))]
        + [
            pltpu.SemaphoreType.DMA((size,))
            for group in ["tokens", "all"] + groups
            for size in (copies(group), copies(group), 1)
        ],
        compiler_params=pltpu.CompilerParams(
            collective_id=collective, has_side_effects=True, vmem_limit_bytes=62 * 1024 * 1024
        ),
        name=name,
    )(outer, query, key, value, mixed, log_total, mask, *kept, *tables, sinks, gain, small)


def close_by(
    tokens,
    segments,
    routes,
    gate_share,
    attn_gain,
    query_weight,
    query_bias,
    key_weight,
    key_bias,
    value_weight,
    value_bias,
    output_weight,
    output_bias,
    sink_logits,
    moe_gain,
    gate_weight,
    gate_bias,
    up_weight,
    up_bias,
    down_weight,
    down_bias,
    cotangent,
):
    count_rows = tokens.shape[1]
    width = tokens.shape[2]
    head_count = sink_logits.shape[0]
    kv_count = key_bias.shape[0] // HD
    group = head_count // kv_count
    experts = lax.axis_size("exp")
    devices = 4 * experts
    topk = routes.shape[2]
    capacity = count_rows * topk * 9 // (8 * experts)
    x, e, y = place_here()
    near_bit = lax.rem(lax.div(e, 2), 2)
    seq_len = 2 * count_rows

    chosen = routes[0].reshape(-1)
    expert_hot = (chosen[:, None] == jnp.arange(experts, dtype=jnp.int32)[None, :]).astype(
        jnp.int32
    )
    earlier = (jnp.cumsum(expert_hot, axis=0) - expert_hot).reshape(count_rows, topk, experts)
    named = expert_hot.reshape(count_rows, topk, experts)
    slot_table = jnp.sum((earlier + 1) * named, axis=1) - 1
    share_table = jnp.sum(named.astype(jnp.float32) * gate_share[0][:, :, None], axis=1)
    table = jnp.concatenate([slot_table.astype(jnp.float32).T, share_table.T], axis=0)

    resid = tokens[0].astype(jnp.float32)
    attn_norm, attn_norm_pull = jax.vjp(rms_apply, resid, attn_gain)
    normed = attn_norm.astype(jnp.bfloat16)
    block_tokens = 4 * count_rows
    held_kv = 2
    held_heads = held_kv * group

    def own_part(vector):
        size = vector.shape[0] // 8
        first = (4 * x + near_bit) * size
        parts = [lax.dynamic_slice(vector, (first + 2 * far * size,), (size,)) for far in range(2)]
        return jnp.concatenate(parts)[None]

    position = jnp.arange(seq_len, dtype=jnp.int32)
    cosine, sine = rope_tables(position, HD)
    cosine = jnp.tile(cosine, (2, 4))
    sine = jnp.tile(jnp.concatenate([-sine, sine], axis=1), (2, 2))
    own_ids = lax.dynamic_slice_in_dim(segments[0], x * count_rows, count_rows, 0)
    marks = jnp.broadcast_to(own_ids.astype(jnp.float32)[:, None], (count_rows, count_rows))
    sinks = own_part(sink_logits)
    (
        attn_out,
        query_rot,
        key_rot,
        value_low,
        mixed,
        log_total,
        mask,
        group_tokens,
        group_query,
        group_key,
        group_value,
        group_output,
        tables,
        all_cotangents,
    ) = attention_forward(
        normed,
        query_weight.T,
        key_weight.T,
        value_weight.T,
        output_weight,
        marks,
        table,
        cotangent[0],
        (own_part(query_bias), own_part(key_bias), own_part(value_bias)),
        (cosine, sine),
        sinks,
        0,
        "attention_forward",
    )
    hidden = resid + (attn_out + output_bias)
    moe_norm, moe_norm_pull = jax.vjp(rms_apply, hidden, moe_gain)
    normed_moe = moe_norm.astype(jnp.bfloat16)

    def by_pairs(part):
        part = jnp.moveaxis(part.reshape(experts, 2, 2, experts, count_rows), 3, 0)
        return part.reshape(experts, experts, 2, 1, 2 * count_rows)

    slots = tables[:, :experts].astype(jnp.int32)
    second_block = jnp.arange(devices, dtype=jnp.int32)[:, None, None] % 2
    seats = by_pairs(jnp.where(slots >= 0, slots + capacity * second_block, -1))
    sibling = e + 1 - 2 * lax.rem(e, 2)
    seats = jnp.stack(
        [
            lax.dynamic_index_in_dim(seats, e, 0, keepdims=False),
            lax.dynamic_index_in_dim(seats, sibling, 0, keepdims=False),
        ]
    )
    gate_rows, up_rows = gate_weight[0].T, up_weight[0].T
    shares = lax.dynamic_index_in_dim(by_pairs(tables[:, experts:]), e, 0, keepdims=False)
    (
        expert_rows,
        grad_rows,
        activation,
        gate_grad,
        up_grad,
        gate_bias_grad,
        up_bias_grad,
        down_bias_grad,
        _,
    ) = expert_rows_kernel(
        normed_moe,
        all_cotangents,
        (gate_rows, up_rows, down_weight[0]),
        (gate_bias, up_bias),
        seats[0],
        shares,
        capacity,
        2,
        "route_rows",
    )
    (normed_moe_grad,) = expert_sums(
        "gradient", (gate_grad, up_grad), (gate_rows, up_rows), seats, (), 3, "sum_rows"
    )
    moe_out, gate_weight_grad, up_weight_grad, down_weight_grad = expert_sums(
        "result",
        (activation,),
        (down_weight[0],),
        seats,
        (shares, down_bias),
        4,
        "sum_results",
        ((gate_grad, expert_rows), (up_grad, expert_rows), (activation, grad_rows)),
    )
    output = (hidden + moe_out).astype(jnp.bfloat16)

    upstream = cotangent[0].astype(jnp.float32)
    hidden_norm_grad, moe_gain_grad = moe_norm_pull(normed_moe_grad)
    hidden_grad = upstream + hidden_norm_grad
    attn_out_grad = hidden_grad.astype(jnp.bfloat16)
    output_bias_grad = jnp.sum(attn_out_grad.astype(jnp.float32), axis=0)
    small = jnp.concatenate(
        [
            jnp.zeros((1, width), jnp.float32),
            moe_gain_grad[None],
            output_bias_grad[None],
            jnp.zeros((5, width), jnp.float32),
        ],
        axis=0,
    )
    query_owned, key_owned, value_owned, output_owned, normed_grad, small_sums = attention_backward(
        attn_out_grad,
        query_rot,
        key_rot,
        value_low,
        mixed,
        log_total,
        mask,
        group_tokens,
        (group_query, group_key, group_value, group_output),
        (cosine, sine),
        sinks,
        attn_gain[None],
        small,
        5,
        "attention_backward",
    )
    lengths = (held_heads * HD, held_kv * HD, held_kv * HD, held_heads)
    resid_norm_grad, _ = attn_norm_pull(normed_grad)
    input_grad = hidden_grad + resid_norm_grad
    pieces = []
    for low, length in zip((0, lengths[0], sum(lengths[:2]), sum(lengths[:3])), lengths):
        piece = small_sums[4:, low : low + length].reshape(2, 2, held_kv, -1)
        pieces.append(jnp.transpose(piece, (1, 2, 0, 3)).reshape(-1))
    query_bias_grad, key_bias_grad, value_bias_grad, sink_grad = pieces
    return (
        output[None],
        input_grad[None],
        small_sums[0],
        query_owned.T,
        query_bias_grad,
        key_owned.T,
        key_bias_grad,
        value_owned.T,
        value_bias_grad,
        output_owned,
        small_sums[2],
        sink_grad,
        small_sums[1],
        gate_weight_grad.T[None],
        gate_bias_grad,
        up_weight_grad.T[None],
        up_bias_grad,
        down_weight_grad[None],
        down_bias_grad,
    )


def solution(mesh):
    placed = (
        P(("exp", "dp"), "seq", None),
        P(("exp", "dp"), None),
        P(("exp", "dp"), "seq", None),
        P(("exp", "dp"), "seq", None),
        P(),
        P(None, ("seq", "exp", "dp")),
        P(),
        P(None, ("seq", "exp", "dp")),
        P(),
        P(None, ("seq", "exp", "dp")),
        P(),
        P(("seq", "exp", "dp"), None),
        P(),
        P(),
        P(),
        P("exp", None, ("seq", "dp")),
        P("exp", ("seq", "dp")),
        P("exp", None, ("seq", "dp")),
        P("exp", ("seq", "dp")),
        P("exp", ("seq", "dp"), None),
        P("exp", None),
        P(("exp", "dp"), "seq", None),
    )
    shape = mesh.shape
    small = shape["seq"] == 2 and shape["dp"] == 2 and shape["exp"] == 8
    return jax.shard_map(
        close_by if small else local,
        mesh=mesh,
        in_specs=placed,
        out_specs=(
            P(("exp", "dp"), "seq", None),
            P(("exp", "dp"), "seq", None),
            P(),
            P(None, ("seq", "exp", "dp")),
            P(),
            P(None, ("seq", "exp", "dp")),
            P(),
            P(None, ("seq", "exp", "dp")),
            P(),
            P(("seq", "exp", "dp"), None),
            P(),
            P(),
            P(),
            P("exp", None, ("seq", "dp")),
            P("exp", ("seq", "dp")),
            P("exp", None, ("seq", "dp")),
            P("exp", ("seq", "dp")),
            P("exp", ("seq", "dp"), None),
            P("exp", None),
        ),
        check_vma=False,
    )
```

profile of v0, /device:TPU:0, one launch (start us, length us, event | category | flops | bytes accessed | tf_op | source)
XLA Modules:
  0.0 794.1 jit_solution(1368500456409847844)
XLA Ops:
  0.7 0.8 fusion.19
  1.5 0.6 pad_maximum_fusion.2
  2.1 0.8 fusion.20
  2.9 0.6 maximum_bitcast_fusion.refs_9_
  4.1 0.8 fusion.22
  4.9 0.6 maximum_bitcast_fusion.2.refs_13_.refs_14_
  5.5 0.7 fusion.12
  6.1 0.7 broadcast_in_dim.65.refs_4_
  6.8 1.5 copy.99
  8.6 1.1 fusion.5.refs_0_
  9.9 1.1 reduce-window.6
  12.6 0.6 pad_maximum_fusion.1.refs_6_
  13.6 0.8 copy.111.refs_12_.refs_13_
  14.5 0.8 copy.110.refs_11_.refs_12_
  15.4 1.2 copy.108
  16.5 1.2 copy.100
  17.7 1.2 copy.109.refs_5_
  18.8 201.7 %attention_forward.1 = (f32[128,2880]{1,0:T(8,128)}, bf16[512,1024]{1,0:T(8,128)(2,1)}, bf16[512,128]{1,0:T(8,128)(2,1)}, bf16[512,128]{1,0:T(8,128)(2,1)}, bf16...) custom-call(bf16[128,2880]{1,0:T(8,128)(2,1)} %fusion.5.refs_0_, ...), custom_call_target="tpu_custom_call" | custom-call | tf_op jit(solution)/shard_map/attention_forward/pallas_call | solution.py:1381
  220.6 1.7 multiply_reduce_fusion.2
  222.3 1.1 multiply_convert_fusion.refs_0_
  223.6 0.6 constant_dynamic-slice_fusion
  224.3 0.6 dynamic-slice_bitcast_fusion.refs_8_.refs_3_
  224.9 133.6 %route_rows.1 = (bf16[2304,2880]{1,0:T(8,128)(2,1)}, bf16[2304,2880]{1,0:T(8,128)(2,1)}, bf16[2304,720]{1,0:T(8,128)(2,1)}, bf16[2304,720]{1,0:T(8,128)(2,1)}, b...) custom-call(bf16[128,2880]{1,0:T(8,128)(2,1)} %multiply_convert_fusi, ...), custom_call_target="tpu_custom_call" | custom-call | tf_op jit(solution)/shard_map/route_rows/pallas_call | solution.py:1039
  358.6 0.6 pad_add_fusion.refs_2_.refs_4_
  359.2 122.8 %sum_results.1 = (f32[128,2880]{1,0:T(8,128)}, f32[720,2880]{1,0:T(8,128)}, f32[720,2880]{1,0:T(8,128)}, f32[720,2880]{1,0:T(8,128)}) custom-call(bf16[2304,720]{1,0:T(8,128)(2,1)} %get-tuple-element.54.refs_0_.refs_9_, bf16[720,2880]{1,0:T(8,128)(2,1)} %bitcast.97, s32[2,8,2,1,256]{4,3,2,1,0:T(1,128)} %pad_add_fusion.refs_2_.refs_4_, ...), custom_call_target="tpu_custom_call" | custom-call | tf_op jit(solution)/shard_map/sum_results/pallas_call | solution.py:848
  482.0 116.9 %sum_rows.1 = f32[128,2880]{1,0:T(8,128)} custom-call(bf16[2304,720]{1,0:T(8,128)(2,1)} %get-tuple-element.55.refs_5_.refs_0_, bf16[2304,720]{1,0:T(8,128)(2,1)} %get-tuple-element.57.refs_7_.refs_1_, bf16[720,2880]{1,0:T(8,128)(2,1)} %bitcast.93, bf16[720,2880]{1,0:T(8,128)(2,1)} %bitcast.95, s32[2,8,2,1,256]{4,3,2,1,0:T(1,128)} %pad_add_fusion.refs_2_.refs_4_), custom_call_target="tpu_custom_call" | custom-call | tf_op jit(solution)/shard_map/sum_rows/pallas_call | solution.py:848
  598.9 2.1 multiply_reduce_fusion
  601.1 1.4 convert_reduce_fusion
  602.6 0.7 maximum_maximum_fusion.refs_16_
  603.3 0.6 broadcast_in_dim.73.refs_15_
  603.9 151.0 %attention_backward.1 = (f32[128,2880]{1,0:T(8,128)}, f32[16,2880]{1,0:T(8,128)}, f32[16,2880]{1,0:T(8,128)}, f32[128,2880]{1,0:T(8,128)}, f32[128,2880]{1,0:T(8,128)}, /*index=5*/f32[8,2880]{1,0:T(8,128)}) custom-call(bf16[128,2880]{1,0:T(8,128)(2,1)} %get-tuple-element.165.refs_0_, bf16[512,1024]{1,0:T(8,128)(2,1)} %get-tuple-element.60.refs_1_, ...), custom_call_target="tpu_custom_call" | custom-call | tf_op jit(solution)/shard_map/attention_backward/pallas_call | solution.py:1656
  755.0 2.0 fusion.6
  757.2 3.9 fusion.2
  761.1 1.6 copy.121
  762.7 1.1 copy.120
  763.8 3.1 copy.122
  766.9 1.6 copy.123
  768.5 0.6 copy.126
  769.1 0.7 slice_reduce_fusion.1
  769.9 0.7 reshape.217
  770.7 0.7 reshape.219
  771.4 0.6 reshape.221
  772.0 0.7 copy.139
  772.7 0.7 copy.140
  773.4 7.8 copy.141
  781.8 7.4 copy.143
  789.8 3.4 copy.145
  793.2 0.6 copy.146
  (106 shorter events, 5.2 us)
Async XLA Ops:
  0.7 7.9 copy-start.12
  8.3 212.3 %copy-start = (bf16[1,128,2880]{2,1,0:T(8,128)(2,1)}, bf16[1,128,2880]{2,1,0:T(8,128)(2,1)S(1)}, u32[]{:S(2)}) copy-start(bf16[1,128,2880]{2,1,0:T(8,128)(2,1)S(1)} %copy.99) | copy-start | bytes 2211844
  8.3 1.4 copy-start.19
  8.6 3.5 copy-start.22
  12.6 2.7 copy-start.7
  14.4 2.1 copy-start.8
  15.4 2.3 copy-start.9
  18.8 201.7 %copy-start.17 = (f32[2880]{0:T(1024)S(1)}, f32[2880]{0:T(1024)}, u32[]{:S(2)}) copy-start(f32[2880]{0:T(1024)} %param.34) | copy-start | bytes 34564
  220.6 1.8 copy-start.11
  222.3 1.1 copy-start.10
  224.9 133.6 %copy-start.15 = (s32[1,8,2,1,256]{4,3,2,1,0:T(1,128)S(1)}, s32[1,8,2,1,256]{4,3,2,1,0:T(1,128)}, u32[]{:S(2)}) copy-start(s32[1,8,2,1,256]{4,3,2,1,0:T(1,128)} %get-tuple-element.171) | copy-start | bytes 49156
  598.9 2.2 copy-start.2
  598.9 2.2 copy-start.4
  754.9 2.0 copy-start.1
  754.9 2.3 copy-start.3
  761.1 1.6 copy-start.5
  763.8 3.1 copy-start.6
  766.9 1.6 copy-start.16
  766.9 5.1 copy-start.14
  766.9 5.8 copy-start.13
  773.4 7.8 copy-start.21
  773.4 16.4 %slice-start = ((s8[8478720]{0:T(1024)(128)(4,1)}), s8[4194304]{0:T(1024)(128)(4,1)S(1)}, s32[]{:S(2)}) async-start(s8[8478720]{0:T(1024)(128)(4,1)} %bitcast.99), calls=%async_computation | async-start | bytes 8388608
  773.4 16.4 %slice-start.1 = ((s8[8478720]{0:T(1024)(128)(4,1)}), s8[4194304]{0:T(1024)(128)(4,1)S(1)}, s32[]{:S(2)}) async-start(s8[8478720]{0:T(1024)(128)(4,1)} %bitcast.99), calls=%async_computation.1 | async-start | bytes 8388608
  781.8 7.4 copy-start.20
  781.8 8.0 %slice-start.2 = ((s8[8478720]{0:T(1024)(128)(4,1)}), s8[90112]{0:T(1024)(128)(4,1)S(1)}, s32[]{:S(2)}) async-start(s8[8478720]{0:T(1024)(128)(4,1)} %bitcast.99), calls=%async_computation.2 | async-start | bytes 180224
  789.8 3.4 copy-start.18
where the time goes:
time: 802 us; the launch traced here: 794 us
  Pallas kernels  726 us (91%)
  local copies, waits for them, and re-layouts  46 us (6%)
  other arithmetic  20.7 us (3%)
    pallas_call x2, Pallas kernels, expert_sums(): pl.pallas_call(body, out_shape=[jax.ShapeDtypeStruct((tokens, width), jnp...  240 us
    pallas_call x1, Pallas kernels, attention_forward(): pl.pallas_call(body, out_shape=[jax.ShapeDtypeStruct((tokens, width), f32...  202 us
    pallas_call x1, Pallas kernels, attention_backward(): pl.pallas_call(body, out_shape=[jax.ShapeDtypeStruct((rows, width), f32)...  151 us
    pallas_call x1, Pallas kernels, expert_rows_kernel(): pl.pallas_call(body, out_shape=[jax.ShapeDtypeStruct((row_count, width),...  134 us
    unnamed x72, local copies, waits for them, and re-layouts  35.1 us

commit v1 on v0

--- a/solution.py
+++ b/solution.py
@@ -1013,8 +1013,8 @@
                 copy.start()
                 thin_copies.append(copy)
 
-        order = ["p0B0B1b0B2b1t0p1r2B3b2c0o0F0b3r3p2t1w0F1f0B4f1c1F2b4"]
-        order += ["p3t2w1F3f2B5f3B6b5c2F4b6w2F5f4t3B7f5b7c3F6w3F7f6f7"]
+        order = ["p0B0B1b0B2b1B3b2B4b3B5b4t0p1r2", "B6b5B7b6b7c0o0F0r3p2f0w0F1f1t1c1"]
+        order += ["p3t2w1F2F3f2f3c2F4w2F5f4f5t3c3F6w3F7f6f7"]
         acts = {
             "p": work.plane,
             "t": work.turn,

time: 802 us -> 805 us (level)
  no operation moved by 1% of the time
where the time goes in v1:
time: 805 us; the launch traced here: 797 us
  Pallas kernels  729 us (91%)
  local copies, waits for them, and re-layouts  46 us (6%)
  other arithmetic  20.7 us (3%)
    pallas_call x2, Pallas kernels, expert_sums(): pl.pallas_call(body, out_shape=[jax.ShapeDtypeStruct((tokens, width), jnp...  238 us
    pallas_call x1, Pallas kernels, attention_forward(): pl.pallas_call(body, out_shape=[jax.ShapeDtypeStruct((tokens, width), f32...  202 us
    pallas_call x1, Pallas kernels, attention_backward(): pl.pallas_call(body, out_shape=[jax.ShapeDtypeStruct((rows, width), f32)...  153 us
    pallas_call x1, Pallas kernels, expert_rows_kernel(): pl.pallas_call(body, out_shape=[jax.ShapeDtypeStruct((row_count, width),...  136 us
    unnamed x72, local copies, waits for them, and re-layouts  35.1 us

profile of v1, /device:TPU:0, one launch (start us, length us, event | category | flops | bytes accessed | tf_op | source)
XLA Modules:
  0.0 797.1 jit_solution(12624239977782678974)
XLA Ops:
  0.7 0.8 fusion.19
  1.5 0.6 pad_maximum_fusion.2
  2.1 0.8 fusion.20
  2.9 0.6 maximum_bitcast_fusion.refs_9_
  4.1 0.8 fusion.22
  4.9 0.6 maximum_bitcast_fusion.2.refs_13_.refs_14_
  5.5 0.7 fusion.12
  6.1 0.7 broadcast_in_dim.65.refs_4_
  6.8 1.5 copy.99
  8.6 1.1 fusion.5.refs_0_
  9.9 1.1 reduce-window.6
  12.6 0.6 pad_maximum_fusion.1.refs_6_
  13.6 0.8 copy.111.refs_12_.refs_13_
  14.5 0.8 copy.110.refs_11_.refs_12_
  15.4 1.2 copy.108
  16.5 1.2 copy.100
  17.7 1.2 copy.109.refs_5_
  18.8 201.7 %attention_forward.1 = (f32[128,2880]{1,0:T(8,128)}, bf16[512,1024]{1,0:T(8,128)(2,1)}, bf16[512,128]{1,0:T(8,128)(2,1)}, bf16[512,128]{1,0:T(8,128)(2,1)}, bf16...) custom-call(bf16[128,2880]{1,0:T(8,128)(2,1)} %fusion.5.refs_0_, ...), custom_call_target="tpu_custom_call" | custom-call | tf_op jit(solution)/shard_map/attention_forward/pallas_call | solution.py:1381
  220.6 1.7 multiply_reduce_fusion.2
  222.3 1.1 multiply_convert_fusion.refs_0_
  223.6 0.6 constant_dynamic-slice_fusion
  224.3 0.6 dynamic-slice_bitcast_fusion.refs_8_.refs_3_
  224.9 136.4 %route_rows.1 = (bf16[2304,2880]{1,0:T(8,128)(2,1)}, bf16[2304,2880]{1,0:T(8,128)(2,1)}, bf16[2304,720]{1,0:T(8,128)(2,1)}, bf16[2304,720]{1,0:T(8,128)(2,1)}, b...) custom-call(bf16[128,2880]{1,0:T(8,128)(2,1)} %multiply_convert_fusi, ...), custom_call_target="tpu_custom_call" | custom-call | tf_op jit(solution)/shard_map/route_rows/pallas_call | solution.py:1039
  361.4 0.6 pad_add_fusion.refs_2_.refs_4_
  362.0 121.6 %sum_results.1 = (f32[128,2880]{1,0:T(8,128)}, f32[720,2880]{1,0:T(8,128)}, f32[720,2880]{1,0:T(8,128)}, f32[720,2880]{1,0:T(8,128)}) custom-call(bf16[2304,720]{1,0:T(8,128)(2,1)} %get-tuple-element.54.refs_0_.refs_9_, bf16[720,2880]{1,0:T(8,128)(2,1)} %bitcast.97, s32[2,8,2,1,256]{4,3,2,1,0:T(1,128)} %pad_add_fusion.refs_2_.refs_4_, ...), custom_call_target="tpu_custom_call" | custom-call | tf_op jit(solution)/shard_map/sum_results/pallas_call | solution.py:848
  483.6 116.4 %sum_rows.1 = f32[128,2880]{1,0:T(8,128)} custom-call(bf16[2304,720]{1,0:T(8,128)(2,1)} %get-tuple-element.55.refs_5_.refs_0_, bf16[2304,720]{1,0:T(8,128)(2,1)} %get-tuple-element.57.refs_7_.refs_1_, bf16[720,2880]{1,0:T(8,128)(2,1)} %bitcast.93, bf16[720,2880]{1,0:T(8,128)(2,1)} %bitcast.95, s32[2,8,2,1,256]{4,3,2,1,0:T(1,128)} %pad_add_fusion.refs_2_.refs_4_), custom_call_target="tpu_custom_call" | custom-call | tf_op jit(solution)/shard_map/sum_rows/pallas_call | solution.py:848
  600.0 2.1 multiply_reduce_fusion
  602.1 1.4 convert_reduce_fusion
  603.6 0.7 maximum_maximum_fusion.refs_16_
  604.4 0.6 broadcast_in_dim.73.refs_15_
  605.0 153.0 %attention_backward.1 = (f32[128,2880]{1,0:T(8,128)}, f32[16,2880]{1,0:T(8,128)}, f32[16,2880]{1,0:T(8,128)}, f32[128,2880]{1,0:T(8,128)}, f32[128,2880]{1,0:T(8,128)}, /*index=5*/f32[8,2880]{1,0:T(8,128)}) custom-call(bf16[128,2880]{1,0:T(8,128)(2,1)} %get-tuple-element.165.refs_0_, bf16[512,1024]{1,0:T(8,128)(2,1)} %get-tuple-element.60.refs_1_, ...), custom_call_target="tpu_custom_call" | custom-call | tf_op jit(solution)/shard_map/attention_backward/pallas_call | solution.py:1656
  758.0 2.0 fusion.6
  760.3 3.9 fusion.2
  764.1 1.6 copy.121
  765.7 1.1 copy.120
  766.9 3.1 copy.122
  769.9 1.6 copy.123
  771.5 0.6 copy.126
  772.2 0.7 slice_reduce_fusion.1
  773.0 0.7 reshape.217
  773.7 0.7 reshape.219
  774.5 0.6 reshape.221
  775.1 0.7 copy.139
  775.7 0.7 copy.140
  776.4 7.8 copy.141
  784.8 7.4 copy.143
  792.8 3.4 copy.145
  796.3 0.6 copy.146
  (106 shorter events, 5.2 us)
Async XLA Ops:
  0.7 7.9 copy-start.12
  8.3 212.3 %copy-start = (bf16[1,128,2880]{2,1,0:T(8,128)(2,1)}, bf16[1,128,2880]{2,1,0:T(8,128)(2,1)S(1)}, u32[]{:S(2)}) copy-start(bf16[1,128,2880]{2,1,0:T(8,128)(2,1)S(1)} %copy.99) | copy-start | bytes 2211844
  8.3 1.4 copy-start.19
  8.6 3.5 copy-start.22
  12.6 2.7 copy-start.7
  14.4 2.1 copy-start.8
  15.4 2.3 copy-start.9
  18.8 201.7 %copy-start.17 = (f32[2880]{0:T(1024)S(1)}, f32[2880]{0:T(1024)}, u32[]{:S(2)}) copy-start(f32[2880]{0:T(1024)} %param.34) | copy-start | bytes 34564
  220.6 1.8 copy-start.11
  222.3 1.1 copy-start.10
  224.9 136.4 %copy-start.15 = (s32[1,8,2,1,256]{4,3,2,1,0:T(1,128)S(1)}, s32[1,8,2,1,256]{4,3,2,1,0:T(1,128)}, u32[]{:S(2)}) copy-start(s32[1,8,2,1,256]{4,3,2,1,0:T(1,128)} %get-tuple-element.171) | copy-start | bytes 49156
  600.0 2.2 copy-start.2
  600.0 2.2 copy-start.4
  758.0 2.0 copy-start.1
  758.0 2.3 copy-start.3
  764.1 1.6 copy-start.5
  766.9 3.1 copy-start.6
  769.9 1.6 copy-start.16
  769.9 5.1 copy-start.14
  769.9 5.8 copy-start.13
  776.4 7.8 copy-start.21
  776.4 16.4 %slice-start = ((s8[8478720]{0:T(1024)(128)(4,1)}), s8[4194304]{0:T(1024)(128)(4,1)S(1)}, s32[]{:S(2)}) async-start(s8[8478720]{0:T(1024)(128)(4,1)} %bitcast.99), calls=%async_computation | async-start | bytes 8388608
  776.4 16.4 %slice-start.1 = ((s8[8478720]{0:T(1024)(128)(4,1)}), s8[4194304]{0:T(1024)(128)(4,1)S(1)}, s32[]{:S(2)}) async-start(s8[8478720]{0:T(1024)(128)(4,1)} %bitcast.99), calls=%async_computation.1 | async-start | bytes 8388608
  784.8 7.4 copy-start.20
  784.8 8.0 %slice-start.2 = ((s8[8478720]{0:T(1024)(128)(4,1)}), s8[90112]{0:T(1024)(128)(4,1)S(1)}, s32[]{:S(2)}) async-start(s8[8478720]{0:T(1024)(128)(4,1)} %bitcast.99), calls=%async_computation.2 | async-start | bytes 180224
  792.8 3.4 copy-start.18
